TPU v7x, 128 devices: a whole 4x4x4 slice. The times are simulated.
128 devices in a mesh: grp: 4 (over y), dev: 32 (over z, x, core).
Axes of the slice: x: 4, y: 4, z: 4, core: 2. Of those that a mesh axis runs over, the one named last changes fastest.
Arguments:
- points: float32 [64, 196608], P(None, 'dev'), may hold values from -6 to 6
- weights: float32 [196608, 128], P('dev'), may hold values from -4 to 4
- proj: float32 [256, 196608], P(None, 'dev'), may hold values from -0.078125 to 0.078125
- fetch_table: int32 [3, 32, 32, 2], P(None, 'dev'), may hold values from 0 to 11, as said below
- near_list: int32 [384, 16], P('dev'), may hold values from 0 to 63, as said below
- far_list: int32 [384, 8], P('dev'), may hold values from 0 to 31, as said below
- skel_idx: int32 [32, 256], P('dev'), may hold values from 0 to 6143, as said below
Outputs:
- potential: float32 [196608, 128], P('dev')
Inputs may be any that keep to these rules, and one draw needn't show every extreme that they name: Entries of fetch_table[r, d, e] are distinct local leaf numbers of column e. `near_list`: the 16 slots of one target leaf are distinct. `far_list`: the 8 nodes of one target leaf are distinct, and one of them is node (c + 1) mod 32 for the leaf's column c. `skel_idx`: the 256 skeleton points of one node are distinct.
All inputs are finite; a program needn't handle non-finite values.
Results may differ from a plain program's by a relative error of at most 0.0003.
Values sent between devices are 32-bit elements; how exact they have to be, the bound alone decides.
A program may use at most 192 MiB of HBM per device.

v0:
```python
import jax
import jax.numpy as jnp
from jax import lax
from jax.sharding import PartitionSpec as P


def kernel_sum(target, sources, values):
    high = lax.Precision.HIGHEST
    inner = jnp.einsum("dt,jds->tjs", target, sources, precision=high)
    target_norm = jnp.sum(target * target, axis=0)
    source_norm = jnp.sum(sources * sources, axis=1)
    distance = target_norm[:, None, None] + source_norm[None] - 2.0 * inner
    kernel = jnp.exp(-distance * (2.0 / target.shape[0]))
    return jnp.einsum("tjs,jsw->tw", kernel, values, precision=high)


def on_device(points, weights, proj, fetch_table, near_list, far_list, skel_idx):
    features, column_points = points.shape
    columns = weights.shape[1]
    devices = lax.axis_size("dev")
    groups = lax.axis_size("grp")
    targets = near_list.shape[0]
    leaf_size = column_points // targets
    row_leaves = targets // (groups - 1)
    capacity = fetch_table.shape[3]
    skeleton = skel_idx.shape[1]
    group_index = lax.axis_index("grp")
    near_row = jnp.minimum(group_index, groups - 2)
    far_side = group_index == groups - 1
    leaf_coords = points.reshape(features, targets, leaf_size)
    leaf_weights = weights.reshape(targets, leaf_size, columns)
    requests = lax.dynamic_index_in_dim(fetch_table[:, 0], near_row, 0, keepdims=False)
    asked = lax.all_to_all(requests, "dev", split_axis=0, concat_axis=0, tiled=True)
    coords = jnp.moveaxis(jnp.take(leaf_coords, asked, axis=1), 0, 2)
    values = jnp.take(leaf_weights, asked, axis=0)
    fetched_coords = lax.all_to_all(coords, "dev", split_axis=0, concat_axis=0, tiled=True)
    fetched_values = lax.all_to_all(values, "dev", split_axis=0, concat_axis=0, tiled=True)
    flat_coords = fetched_coords.reshape(devices * capacity, features, leaf_size)
    flat_values = fetched_values.reshape(devices * capacity, leaf_size, columns)
    local_skeleton = jnp.take(points, skel_idx[0], axis=1)
    share_len = column_points // groups
    share_start = group_index * share_len
    share_proj = lax.dynamic_slice_in_dim(proj, share_start, share_len, 1)
    share_weights = lax.dynamic_slice_in_dim(weights, share_start, share_len, 0)
    partial_value = jnp.dot(
        share_proj,
        share_weights,
        preferred_element_type=jnp.float32,
        precision=lax.Precision.HIGHEST,
    )
    node_index = lax.axis_index("dev")
    owner_mask = jnp.where(far_side, 1.0, 0.0).astype(jnp.float32)
    table_coords = jnp.zeros((devices, features, skeleton), jnp.float32)
    table_coords = lax.dynamic_update_index_in_dim(
        table_coords, local_skeleton * owner_mask, node_index, 0
    )
    table_weights = jnp.zeros((devices, skeleton, columns), jnp.float32)
    table_weights = lax.dynamic_update_index_in_dim(table_weights, partial_value, node_index, 0)
    skel_coords, skel_weights = lax.psum((table_coords, table_weights), ("grp", "dev"))

    def near_work():
        slots = lax.dynamic_slice_in_dim(near_list, near_row * row_leaves, row_leaves, 0)
        leaf_numbers = near_row * row_leaves + jnp.arange(row_leaves, dtype=jnp.int32)

        def near_leaf(items):
            leaf_number, leaf_slots = items
            target = jnp.take(leaf_coords, leaf_number, axis=1)
            return kernel_sum(
                target,
                jnp.take(flat_coords, leaf_slots, axis=0),
                jnp.take(flat_values, leaf_slots, axis=0),
            )

        block = lax.map(near_leaf, (leaf_numbers, slots))
        empty = jnp.zeros((targets, leaf_size, columns), jnp.float32)
        return lax.dynamic_update_slice_in_dim(empty, block, near_row * row_leaves, 0)

    def far_work():

        def far_leaf(items):
            leaf_number, node_ids = items
            target = jnp.take(leaf_coords, leaf_number, axis=1)
            return kernel_sum(
                target,
                jnp.take(skel_coords, node_ids, axis=0),
                jnp.take(skel_weights, node_ids, axis=0),
            )

        return lax.map(far_leaf, (jnp.arange(targets, dtype=jnp.int32), far_list))

    contribution = lax.cond(far_side, far_work, near_work)
    total = lax.psum(contribution, "grp")
    return total.reshape(column_points, columns)


def solution(mesh):
    placed = (
        P(None, "dev"),
        P("dev", None),
        P(None, "dev"),
        P(None, "dev", None, None),
        P("dev", None),
        P("dev", None),
        P("dev", None),
    )
    return jax.shard_map(
        on_device, mesh=mesh, in_specs=placed, out_specs=P("dev", None), check_vma=False
    )
```

profile of v0, /device:TPU:1, one launch (start us, length us, event | category | flops | bytes accessed | tf_op | source)
XLA Modules:
  0.0 820.4 jit_solution(13350892789192930071)
XLA Ops:
  6.5 0.8 fusion.82
  7.4 0.7 copy.36
  8.1 9.4 %all-to-all-start = ((s32[32,1,2]{2,1,0:T(1,128)}), s32[32,1,2]{2,1,0:T(1,128)S(1)}, u32[]{:S(2)}, u32[]{:S(2)}) async-start(s32[32,1,2]{2,1,0:T(1,128)} %copy.36), calls=%async_computation | async-start | bytes 32768 | tf_op jit(solution)/shard_map/all_to_all | solution.py:33
  17.5 2.7 copy.64
  20.2 4.2 all-to-all-done
  24.8 5.7 gather_fusion.4
  30.6 8.5 %broadcast_select_fusion.1 = f32[32,2,64,512]{3,2,1,0:T(8,128)} fusion(f32[32,2,64,512]{3,2,1,0:T(8,128)} %bitcast.103, pred[32,2]{1,0:T(8,128)(4,1)S(1)} %copy.38), kind=kLoop, calls=%fused_computation.87 | loop fusion | flops 2097152 | bytes 16777280 | tf_op jit(solution)/shard_map/jit(_take)/select_n | solution.py:34
  39.1 5.2 all-to-all-start.1
  44.3 7.4 gather_fusion.5
  51.6 11.6 %broadcast_select_fusion = f32[32,2,512,128]{3,2,1,0:T(8,128)} fusion(f32[32,2,512,128]{3,2,1,0:T(8,128)} %bitcast.101, pred[32,2]{1,0:T(8,128)(4,1)S(1)} %copy.38), kind=kLoop, calls=%fused_computation.86 | loop fusion | flops 4194304 | bytes 33554496 | tf_op jit(solution)/shard_map/jit(_take)/select_n | solution.py:35
  63.2 80.8 %all-to-all-done.1 = f32[32,2,64,512]{3,2,1,0:T(8,128)} async-done(((f32[32,2,64,512]{3,2,1,0:T(8,128)}), f32[32,2,64,512]{3,2,1,0:T(8,128)}, u32[]{:S(2)}, u32[]{:S(2)}) %all-to-all-start.1) | async-done | bytes 8388640 | tf_op jit(solution)/shard_map/all_to_all | solution.py:36
  144.0 11.3 %all-to-all-start.2 = ((f32[32,2,512,128]{3,2,1,0:T(8,128)}), f32[32,2,512,128]{3,2,1,0:T(8,128)}, u32[]{:S(2)}, u32[]{:S(2)}) async-start(f32[32,2,512,128]{3,2,1,0:T(8,128)} %broadcast_select_fusion), calls=%async_computation.2 | async-start | bytes 33554432 | tf_op jit(solution)/shard_map/all_to_all | solution.py:37
  155.4 3.3 copy.43
  158.6 2.6 gather_fusion.6
  161.3 2.4 broadcast_in_dim.110
  163.8 3.5 fusion.75
  167.2 1.6 broadcast_in_dim.107
  168.8 0.6 fusion.80
  169.5 1.9 reshape.193
  171.4 310.3 %all-reduce.6.cloned.1.call-done = (f32[32,64,256]{2,1,0:T(8,128)}, f32[32,256,128]{2,1,0:T(8,128)}) async-done(((f32[32,64,256]{2,1,0:T(8,128)}, f32[32,256,128]{2,1,0:T(8,128)}), (f32[32,64,256]{2,1,0:T(8,128)}, f32[32,256,128]{2,1,0:T(8,128)})) %all-reduce.6.cloned.1.call-update) | async-done | bytes 6291472 | tf_op jit(solution)/shard_map/psum | solution.py:59
  481.8 223.2 %conditional.1 = (f32[12,512,128]{2,1,0:T(8,128)}) conditional(s32[]{:T(128)} %convert_element_type.3, (s32[]{:T(128)}, s32[12,16]{1,0:T(8,128)}, f32[32,2,64,512]{3,2,1,0:T(8,128)}, f32[32,2,512,128]{3,2,1,0:T(8,128)}, f32[64,12,512]{2,1,0:T(8,128)}) %tuple.20, (f32[64,12,512]{2,1,0:T(8,128)}, s32[12,8]{0,1:T(8,128)S(1)}, f32[32,64,256]{2,1,0:T(8,128)}, ...), branch_computations={%region_2.0_spmd, %region_7.13_spmd} | conditional | flops 9687917568 | bytes 60630836 | solution.py:91
  481.8 0.7 constant_dynamic-slice_fusion.2
  482.4 218.3 %while.19 = (s32[]{:T(128)}, f32[4,512,128]{2,1,0:T(8,128)}, s32[4]{0:T(128)S(1)}, f32[64,12,512]{2,1,0:T(8,128)}, s32[4,16]{1,0:T(4,128)S(1)}, /*index=5*/f32[6...) while((s32[]{:T(128)}, f32[4,512,128]{2,1,0:T(8,128)}, ...), condition=%wide.region_6.7_spmd, body=%wide.region_3.6_spmd.sunk | while | flops 9687917568 | bytes 55387260 | solution.py:74
  482.5 0.6 dynamic_slice.65
  484.9 1.3 constant_dynamic-slice_fusion.9
  486.3 4.1 gather_fusion.3
  490.4 16.2 %fusion.112 = f32[512,16,512]{2,0,1:T(8,128)} fusion(f32[16,64,512]{2,1,0:T(8,128)S(1)} %gather_fusion.3, pred[16]{0:T(512)(128)(4,1)S(1)} %compare_and_fusion.7, f32[64,1,512]{2,1,0:T(1,128)S(1)} %constant_dynamic-slice_fusion.9, pred[]{:T(512)S(6)} %and.57), kind=kOutput, calls=%fused_computation.22.clone.1 | convolution fusion | flops 3221782528 | bytes 19005456 | tf_op jit(solution)/shard_map/cond/branch_0_fun/while/body/eval_jaxpr/dt,jds->tjs/dot_general | solution.py:9
  507.0 8.5 %gather_fusion.2 = f32[16,512,128]{2,1,0:T(8,128)} fusion(f32[64,512,128]{2,1,0:T(8,128)} %get-tuple-element.330, s32[1024]{0:T(1024)S(1)} %pad_clamp_fusion.7), kind=kCustom, calls=%fused_computation.1.clone.1 | custom fusion | bytes 8388672 | tf_op jit(solution)/shard_map/cond/branch_0_fun/while/body/eval_jaxpr/jit(_take)/gather | solution.py:71
  515.5 21.5 %fusion.114 = f32[4,512,128]{2,1,0:T(8,128)} fusion(f32[4,512,128]{2,1,0:T(8,128)} %get-tuple-element.314, s32[]{:T(128)} %get-tuple-element.313, f32[16,512,128]{2,1,0:T(8,128)} %gather_fusion.2, pred[16]{0:T(512)(128)(4,1)S(1)} %compare_and_fusion.7, f32[512,16,512]{2,0,1:T(8,128)} %fusion.112, f32[16,512]{1,0:T(8,128)S(1)} %multiply_reduce_fusion.5, ...), kind=kOutput, calls=%fused_computation.25.clone.1 | convolution fusion | flops 6464471040 | bytes 21269008 | tf_op jit(solution)/shard_map/cond/branch_0_fun/while/body/eval_jaxpr/tjs,jsw->tw/dot_general | solution.py:14
  539.5 1.3 constant_dynamic-slice_fusion.9
  540.9 4.1 gather_fusion.3
  545.0 16.2 %fusion.112 = f32[512,16,512]{2,0,1:T(8,128)} fusion(f32[16,64,512]{2,1,0:T(8,128)S(1)} %gather_fusion.3, pred[16]{0:T(512)(128)(4,1)S(1)} %compare_and_fusion.7, f32[64,1,512]{2,1,0:T(1,128)S(1)} %constant_dynamic-slice_fusion.9, pred[]{:T(512)S(6)} %and.57), kind=kOutput, calls=%fused_computation.22.clone.1 | convolution fusion | flops 3221782528 | bytes 19005456 | tf_op jit(solution)/shard_map/cond/branch_0_fun/while/body/eval_jaxpr/dt,jds->tjs/dot_general | solution.py:9
  561.5 8.5 %gather_fusion.2 = f32[16,512,128]{2,1,0:T(8,128)} fusion(f32[64,512,128]{2,1,0:T(8,128)} %get-tuple-element.330, s32[1024]{0:T(1024)S(1)} %pad_clamp_fusion.7), kind=kCustom, calls=%fused_computation.1.clone.1 | custom fusion | bytes 8388672 | tf_op jit(solution)/shard_map/cond/branch_0_fun/while/body/eval_jaxpr/jit(_take)/gather | solution.py:71
  570.1 21.5 %fusion.114 = f32[4,512,128]{2,1,0:T(8,128)} fusion(f32[4,512,128]{2,1,0:T(8,128)} %get-tuple-element.314, s32[]{:T(128)} %get-tuple-element.313, f32[16,512,128]{2,1,0:T(8,128)} %gather_fusion.2, pred[16]{0:T(512)(128)(4,1)S(1)} %compare_and_fusion.7, f32[512,16,512]{2,0,1:T(8,128)} %fusion.112, f32[16,512]{1,0:T(8,128)S(1)} %multiply_reduce_fusion.5, ...), kind=kOutput, calls=%fused_computation.25.clone.1 | convolution fusion | flops 6464471040 | bytes 21269008 | tf_op jit(solution)/shard_map/cond/branch_0_fun/while/body/eval_jaxpr/tjs,jsw->tw/dot_general | solution.py:14
  594.1 1.3 constant_dynamic-slice_fusion.9
  595.4 4.1 gather_fusion.3
  599.5 16.2 %fusion.112 = f32[512,16,512]{2,0,1:T(8,128)} fusion(f32[16,64,512]{2,1,0:T(8,128)S(1)} %gather_fusion.3, pred[16]{0:T(512)(128)(4,1)S(1)} %compare_and_fusion.7, f32[64,1,512]{2,1,0:T(1,128)S(1)} %constant_dynamic-slice_fusion.9, pred[]{:T(512)S(6)} %and.57), kind=kOutput, calls=%fused_computation.22.clone.1 | convolution fusion | flops 3221782528 | bytes 19005456 | tf_op jit(solution)/shard_map/cond/branch_0_fun/while/body/eval_jaxpr/dt,jds->tjs/dot_general | solution.py:9
  616.1 8.5 %gather_fusion.2 = f32[16,512,128]{2,1,0:T(8,128)} fusion(f32[64,512,128]{2,1,0:T(8,128)} %get-tuple-element.330, s32[1024]{0:T(1024)S(1)} %pad_clamp_fusion.7), kind=kCustom, calls=%fused_computation.1.clone.1 | custom fusion | bytes 8388672 | tf_op jit(solution)/shard_map/cond/branch_0_fun/while/body/eval_jaxpr/jit(_take)/gather | solution.py:71
  624.6 21.5 %fusion.114 = f32[4,512,128]{2,1,0:T(8,128)} fusion(f32[4,512,128]{2,1,0:T(8,128)} %get-tuple-element.314, s32[]{:T(128)} %get-tuple-element.313, f32[16,512,128]{2,1,0:T(8,128)} %gather_fusion.2, pred[16]{0:T(512)(128)(4,1)S(1)} %compare_and_fusion.7, f32[512,16,512]{2,0,1:T(8,128)} %fusion.112, f32[16,512]{1,0:T(8,128)S(1)} %multiply_reduce_fusion.5, ...), kind=kOutput, calls=%fused_computation.25.clone.1 | convolution fusion | flops 6464471040 | bytes 21269008 | tf_op jit(solution)/shard_map/cond/branch_0_fun/while/body/eval_jaxpr/tjs,jsw->tw/dot_general | solution.py:14
  648.6 1.3 constant_dynamic-slice_fusion.9
  650.0 4.1 gather_fusion.3
  654.1 16.2 %fusion.112 = f32[512,16,512]{2,0,1:T(8,128)} fusion(f32[16,64,512]{2,1,0:T(8,128)S(1)} %gather_fusion.3, pred[16]{0:T(512)(128)(4,1)S(1)} %compare_and_fusion.7, f32[64,1,512]{2,1,0:T(1,128)S(1)} %constant_dynamic-slice_fusion.9, pred[]{:T(512)S(6)} %and.57), kind=kOutput, calls=%fused_computation.22.clone.1 | convolution fusion | flops 3221782528 | bytes 19005456 | tf_op jit(solution)/shard_map/cond/branch_0_fun/while/body/eval_jaxpr/dt,jds->tjs/dot_general | solution.py:9
  670.7 8.5 %gather_fusion.2 = f32[16,512,128]{2,1,0:T(8,128)} fusion(f32[64,512,128]{2,1,0:T(8,128)} %get-tuple-element.330, s32[1024]{0:T(1024)S(1)} %pad_clamp_fusion.7), kind=kCustom, calls=%fused_computation.1.clone.1 | custom fusion | bytes 8388672 | tf_op jit(solution)/shard_map/cond/branch_0_fun/while/body/eval_jaxpr/jit(_take)/gather | solution.py:71
  679.2 21.5 %fusion.114 = f32[4,512,128]{2,1,0:T(8,128)} fusion(f32[4,512,128]{2,1,0:T(8,128)} %get-tuple-element.314, s32[]{:T(128)} %get-tuple-element.313, f32[16,512,128]{2,1,0:T(8,128)} %gather_fusion.2, pred[16]{0:T(512)(128)(4,1)S(1)} %compare_and_fusion.7, f32[512,16,512]{2,0,1:T(8,128)} %fusion.112, f32[16,512]{1,0:T(8,128)S(1)} %multiply_reduce_fusion.5, ...), kind=kOutput, calls=%fused_computation.25.clone.1 | convolution fusion | flops 6464471040 | bytes 21269008 | tf_op jit(solution)/shard_map/cond/branch_0_fun/while/body/eval_jaxpr/tjs,jsw->tw/dot_general | solution.py:14
  700.7 2.0 broadcast.190
  702.7 2.3 constant_dynamic-update-slice_fusion
  705.0 104.8 %all-reduce.4.cloned.1.call-done = f32[6144,128]{1,0:T(8,128)} async-done(((f32[6144,128]{1,0:T(8,128)}), f32[6144,128]{1,0:T(8,128)}) %all-reduce.4.cloned.1.call-update) | async-done | bytes 3145744 | tf_op jit(solution)/shard_map/psum | solution.py:92
  809.8 3.8 copy.95
  (51 shorter events, 4.2 us)
Async XLA Ops:
  6.5 37.7 %copy-start = (f32[6144,128]{1,0:T(8,128)S(1)}, f32[6144,128]{1,0:T(8,128)}, u32[]{:S(2)}) copy-start(f32[6144,128]{1,0:T(8,128)} %param.16) | copy-start | bytes 9437188
  8.1 16.4 %all-to-all-start = ((s32[32,1,2]{2,1,0:T(1,128)}), s32[32,1,2]{2,1,0:T(1,128)S(1)}, u32[]{:S(2)}, u32[]{:S(2)}) async-start(s32[32,1,2]{2,1,0:T(1,128)} %copy.36), calls=%async_computation | async-start | bytes 32768 | tf_op jit(solution)/shard_map/all_to_all | solution.py:33
  39.1 105.0 %all-to-all-start.1 = ((f32[32,2,64,512]{3,2,1,0:T(8,128)}), f32[32,2,64,512]{3,2,1,0:T(8,128)}, u32[]{:S(2)}, u32[]{:S(2)}) async-start(f32[32,2,64,512]{3,2,1,0:T(8,128)} %broadcast_select_fusion.1), calls=%async_computation.1 | async-start | bytes 16777216 | tf_op jit(solution)/shard_map/all_to_all | solution.py:36
  144.0 337.7 %all-to-all-start.2 = ((f32[32,2,512,128]{3,2,1,0:T(8,128)}), f32[32,2,512,128]{3,2,1,0:T(8,128)}, u32[]{:S(2)}, u32[]{:S(2)}) async-start(f32[32,2,512,128]{3,2,1,0:T(8,128)} %broadcast_select_fusion), calls=%async_computation.2 | async-start | bytes 33554432 | tf_op jit(solution)/shard_map/all_to_all | solution.py:37
  155.3 3.3 copy-start.4
  155.3 326.4 %all-reduce.6.cloned.1.call-start = ((), (), s32[]{:S(2)}) async-start(), calls=%async_computation.4 | async-start | bytes 12582912 | tf_op jit(solution)/shard_map/psum | solution.py:59
  167.2 2.3 copy-start.2
  169.4 312.3 %copy-start.3 = (s32[12,8]{0,1:T(8,128)S(1)}, s32[12,8]{0,1:T(8,128)}, u32[]{:S(2)}) copy-start(s32[12,8]{0,1:T(8,128)} %param.20) | copy-start | bytes 1156
  169.5 640.3 %all-reduce.4.cloned.1.call-start = ((), (), s32[]{:S(2)}) async-start(), calls=%async_computation.3 | async-start | bytes 6291456 | tf_op jit(solution)/shard_map/psum | solution.py:92
  705.0 108.6 %copy-start.1 = (f32[6144,128]{1,0:T(8,128)S(1)}, f32[6144,128]{1,0:T(8,128)}, u32[]{:S(2)}) copy-start(f32[6144,128]{1,0:T(8,128)} %param.16) | copy-start | bytes 9437188
Sparse Core Ops, SparseCore 0:
  169.6 312.1 all-reduce.5
  705.1 104.6 all-reduce.3
where the time goes:
time: 823 us; the launch traced here: 820 us
  waiting for transfers between devices  500 us (61%)
  matrix products  154 us (19%)
  local copies, waits for them, and re-layouts  96.2 us (12%)
  starting transfers between devices  26 us (3%)
  other arithmetic  22.5 us (3%)
  between operations  13.5 us (2%)
    psum x1, waiting for transfers between devices, on_device(): lax.psum((table_coords, table_weights), ('grp', 'dev'))  310 us
    psum x1, waiting for transfers between devices, on_device(): total = lax.psum(contribution, 'grp')  105 us
    dot_general x4, matrix products, kernel_sum(): return jnp.einsum('tjs,jsw->tw', kernel, values, precision=high)  86.1 us
    all_to_all x1, waiting for transfers between devices, on_device(): lax.all_to_all(coords, 'dev', split_axis=0, concat_axis=0, tiled=True)  80.8 us
    dot_general x4, matrix products, kernel_sum(): inner = jnp.einsum('dt,jds->tjs', target, sources, precision=high)  64.7 us
    gather x4, local copies, waits for them, and re-layouts, near_leaf(): jnp.take(flat_values, leaf_slots, axis=0)  34 us
  transfers between devices with their start and end apart: 5, of which 4 were waited for; matrix products, arithmetic and copies ran while one was open for 5% of the time, Pallas kernels for 0%

commit v1 on v0

--- a/solution.py
+++ b/solution.py
@@ -2,6 +2,11 @@
 import jax.numpy as jnp
 from jax import lax
 from jax.sharding import PartitionSpec as P
+
+
+def one_after_other(x, one, other):
+    half = lax.psum(x, one)
+    return lax.psum(half, other)
 
 
 def kernel_sum(target, sources, values):
@@ -56,7 +61,7 @@
     )
     table_weights = jnp.zeros((devices, skeleton, columns), jnp.float32)
     table_weights = lax.dynamic_update_index_in_dim(table_weights, partial_value, node_index, 0)
-    skel_coords, skel_weights = lax.psum((table_coords, table_weights), ("grp", "dev"))
+    skel_coords, skel_weights = one_after_other((table_coords, table_weights), "dev", "grp")
 
     def near_work():
         slots = lax.dynamic_slice_in_dim(near_list, near_row * row_leaves, row_leaves, 0)

time: 823 us -> 922 us (1.12)
  waiting for transfers between devices: 500 us -> 600 us
    psum x1 -> x2, waiting for transfers between devices: 310 us -> 408 us  [the longest x1 281 us: one_after_other(): half = lax.psum(x, one)]
  transfers between devices with their start and end apart: 5 -> 6, of which waited for: 4 -> 5; matrix products, arithmetic and copies ran while one was open for 5% -> 4% of each run, Pallas kernels for 0% -> 0%
where the time goes in v1:
time: 922 us; the launch traced here: 920 us
  waiting for transfers between devices  600 us (65%)
  matrix products  154 us (17%)
  local copies, waits for them, and re-layouts  96.3 us (10%)
  starting transfers between devices  26 us (3%)
  other arithmetic  21.9 us (2%)
  between operations  13.2 us (1%)
    psum x1, waiting for transfers between devices, one_after_other(): half = lax.psum(x, one)  281 us
    psum x1, waiting for transfers between devices, one_after_other(): return lax.psum(half, other)  127 us
    psum x1, waiting for transfers between devices, on_device(): total = lax.psum(contribution, 'grp')  107 us
    dot_general x4, matrix products, kernel_sum(): return jnp.einsum('tjs,jsw->tw', kernel, values, precision=high)  86.1 us
    all_to_all x1, waiting for transfers between devices, on_device(): lax.all_to_all(coords, 'dev', split_axis=0, concat_axis=0, tiled=True)  80.8 us
    dot_general x4, matrix products, kernel_sum(): inner = jnp.einsum('dt,jds->tjs', target, sources, precision=high)  64.8 us
    gather x4, local copies, waits for them, and re-layouts, near_leaf(): jnp.take(flat_values, leaf_slots, axis=0)  34 us
  transfers between devices with their start and end apart: 6, of which 5 were waited for; matrix products, arithmetic and copies ran while one was open for 4% of the time, Pallas kernels for 0%

profile of v1, /device:TPU:1, one launch (start us, length us, event | category | flops | bytes accessed | tf_op | source)
XLA Modules:
  0.0 919.9 jit_solution(17287666366126362514)
XLA Ops:
  6.5 0.8 fusion.82
  7.4 0.7 copy.36
  8.1 9.4 %all-to-all-start = ((s32[32,1,2]{2,1,0:T(1,128)}), s32[32,1,2]{2,1,0:T(1,128)S(1)}, u32[]{:S(2)}, u32[]{:S(2)}) async-start(s32[32,1,2]{2,1,0:T(1,128)} %copy.36), calls=%async_computation | async-start | bytes 32768 | tf_op jit(solution)/shard_map/all_to_all | solution.py:38
  17.5 2.7 copy.64
  20.2 4.2 all-to-all-done
  24.8 5.7 gather_fusion.4
  30.6 8.5 broadcast_select_fusion.1
  39.1 5.2 all-to-all-start.1
  44.3 7.4 gather_fusion.5
  51.6 11.6 %broadcast_select_fusion = f32[32,2,512,128]{3,2,1,0:T(8,128)} fusion(f32[32,2,512,128]{3,2,1,0:T(8,128)} %bitcast.101, pred[32,2]{1,0:T(8,128)(4,1)S(1)} %copy.38), kind=kLoop, calls=%fused_computation.86 | loop fusion | flops 4194304 | bytes 33554496 | tf_op jit(solution)/shard_map/jit(_take)/select_n | solution.py:40
  63.2 80.8 %all-to-all-done.1 = f32[32,2,64,512]{3,2,1,0:T(8,128)} async-done(((f32[32,2,64,512]{3,2,1,0:T(8,128)}), f32[32,2,64,512]{3,2,1,0:T(8,128)}, u32[]{:S(2)}, u32[]{:S(2)}) %all-to-all-start.1) | async-done | bytes 8388640 | tf_op jit(solution)/shard_map/all_to_all | solution.py:41
  144.0 11.3 %all-to-all-start.2 = ((f32[32,2,512,128]{3,2,1,0:T(8,128)}), f32[32,2,512,128]{3,2,1,0:T(8,128)}, u32[]{:S(2)}, u32[]{:S(2)}) async-start(f32[32,2,512,128]{3,2,1,0:T(8,128)} %broadcast_select_fusion), calls=%async_computation.2 | async-start | bytes 33554432 | tf_op jit(solution)/shard_map/all_to_all | solution.py:42
  155.4 3.3 copy.43
  158.7 2.6 gather_fusion.6
  161.4 2.4 broadcast_in_dim.110
  163.8 3.5 fusion.75
  167.6 1.3 copy-done.3
  169.0 280.7 %all-reduce.8.cloned.1.call-done = (f32[32,64,256]{2,1,0:T(8,128)}, f32[32,256,128]{2,1,0:T(8,128)}) async-done(((f32[32,64,256]{2,1,0:T(8,128)}, f32[32,256,128]{2,1,0:T(8,128)}), (f32[32,64,256]{2,1,0:T(8,128)}, f32[32,256,128]{2,1,0:T(8,128)})) %all-reduce.8.cloned.1.call-update) | async-done | bytes 6291472 | tf_op jit(solution)/shard_map/psum | solution.py:8
  449.8 1.9 reshape.193
  451.7 127.1 %all-reduce.10.cloned.1.call-done = (f32[32,64,256]{2,1,0:T(8,128)}, f32[32,256,128]{2,1,0:T(8,128)}) async-done(((f32[32,64,256]{2,1,0:T(8,128)}, f32[32,256,128]{2,1,0:T(8,128)}), (f32[32,64,256]{2,1,0:T(8,128)}, f32[32,256,128]{2,1,0:T(8,128)})) %all-reduce.10.cloned.1.call-update) | async-done | bytes 6291472 | tf_op jit(solution)/shard_map/psum | solution.py:9
  578.8 223.3 %conditional.1 = (f32[12,512,128]{2,1,0:T(8,128)}) conditional(s32[]{:T(128)} %convert_element_type.3, (s32[]{:T(128)}, s32[12,16]{1,0:T(8,128)}, f32[32,2,64,512]{3,2,1,0:T(8,128)}, f32[32,2,512,128]{3,2,1,0:T(8,128)}, f32[64,12,512]{2,1,0:T(8,128)}) %tuple.20, (f32[64,12,512]{2,1,0:T(8,128)}, s32[12,8]{0,1:T(8,128)S(1)}, ...), branch_computations={%region_4.10_spmd, %region_9.15_spmd} | conditional | flops 9687917568 | bytes 60630836 | solution.py:96
  578.8 0.7 constant_dynamic-slice_fusion.2
  579.5 218.4 %while.19 = (s32[]{:T(128)}, f32[4,512,128]{2,1,0:T(8,128)}, s32[4]{0:T(128)S(1)}, f32[64,12,512]{2,1,0:T(8,128)}, s32[4,16]{1,0:T(4,128)S(1)}, /*index=5*/f32[6...) while((s32[]{:T(128)}, f32[4,512,128]{2,1,0:T(8,128)}, ...), condition=%wide.region_8.9_spmd, body=%wide.region_5.8_spmd.sunk | while | flops 9687917568 | bytes 55387260 | solution.py:79
  579.5 0.6 dynamic_slice.65
  582.0 1.3 constant_dynamic-slice_fusion.9
  583.3 4.1 gather_fusion.3
  587.4 16.2 %fusion.112 = f32[512,16,512]{2,0,1:T(8,128)} fusion(f32[16,64,512]{2,1,0:T(8,128)S(1)} %gather_fusion.3, pred[16]{0:T(512)(128)(4,1)S(1)} %compare_and_fusion.7, f32[64,1,512]{2,1,0:T(1,128)S(1)} %constant_dynamic-slice_fusion.9, pred[]{:T(512)S(6)} %and.57), kind=kOutput, calls=%fused_computation.22.clone.1 | convolution fusion | flops 3221782528 | bytes 19005456 | tf_op jit(solution)/shard_map/cond/branch_0_fun/while/body/eval_jaxpr/dt,jds->tjs/dot_general | solution.py:14
  604.0 8.5 gather_fusion.2
  612.5 21.5 %fusion.114 = f32[4,512,128]{2,1,0:T(8,128)} fusion(f32[4,512,128]{2,1,0:T(8,128)} %get-tuple-element.316, s32[]{:T(128)} %get-tuple-element.315, f32[16,512,128]{2,1,0:T(8,128)} %gather_fusion.2, pred[16]{0:T(512)(128)(4,1)S(1)} %compare_and_fusion.7, f32[512,16,512]{2,0,1:T(8,128)} %fusion.112, f32[16,512]{1,0:T(8,128)S(1)} %multiply_reduce_fusion.5, ...), kind=kOutput, calls=%fused_computation.25.clone.1 | convolution fusion | flops 6464471040 | bytes 21269008 | tf_op jit(solution)/shard_map/cond/branch_0_fun/while/body/eval_jaxpr/tjs,jsw->tw/dot_general | solution.py:19
  636.5 1.3 constant_dynamic-slice_fusion.9
  637.9 4.1 gather_fusion.3
  642.0 16.2 %fusion.112 = f32[512,16,512]{2,0,1:T(8,128)} fusion(f32[16,64,512]{2,1,0:T(8,128)S(1)} %gather_fusion.3, pred[16]{0:T(512)(128)(4,1)S(1)} %compare_and_fusion.7, f32[64,1,512]{2,1,0:T(1,128)S(1)} %constant_dynamic-slice_fusion.9, pred[]{:T(512)S(6)} %and.57), kind=kOutput, calls=%fused_computation.22.clone.1 | convolution fusion | flops 3221782528 | bytes 19005456 | tf_op jit(solution)/shard_map/cond/branch_0_fun/while/body/eval_jaxpr/dt,jds->tjs/dot_general | solution.py:14
  658.6 8.5 gather_fusion.2
  667.1 21.5 %fusion.114 = f32[4,512,128]{2,1,0:T(8,128)} fusion(f32[4,512,128]{2,1,0:T(8,128)} %get-tuple-element.316, s32[]{:T(128)} %get-tuple-element.315, f32[16,512,128]{2,1,0:T(8,128)} %gather_fusion.2, pred[16]{0:T(512)(128)(4,1)S(1)} %compare_and_fusion.7, f32[512,16,512]{2,0,1:T(8,128)} %fusion.112, f32[16,512]{1,0:T(8,128)S(1)} %multiply_reduce_fusion.5, ...), kind=kOutput, calls=%fused_computation.25.clone.1 | convolution fusion | flops 6464471040 | bytes 21269008 | tf_op jit(solution)/shard_map/cond/branch_0_fun/while/body/eval_jaxpr/tjs,jsw->tw/dot_general | solution.py:19
  691.1 1.3 constant_dynamic-slice_fusion.9
  692.5 4.1 gather_fusion.3
  696.6 16.2 %fusion.112 = f32[512,16,512]{2,0,1:T(8,128)} fusion(f32[16,64,512]{2,1,0:T(8,128)S(1)} %gather_fusion.3, pred[16]{0:T(512)(128)(4,1)S(1)} %compare_and_fusion.7, f32[64,1,512]{2,1,0:T(1,128)S(1)} %constant_dynamic-slice_fusion.9, pred[]{:T(512)S(6)} %and.57), kind=kOutput, calls=%fused_computation.22.clone.1 | convolution fusion | flops 3221782528 | bytes 19005456 | tf_op jit(solution)/shard_map/cond/branch_0_fun/while/body/eval_jaxpr/dt,jds->tjs/dot_general | solution.py:14
  713.2 8.5 gather_fusion.2
  721.7 21.5 %fusion.114 = f32[4,512,128]{2,1,0:T(8,128)} fusion(f32[4,512,128]{2,1,0:T(8,128)} %get-tuple-element.316, s32[]{:T(128)} %get-tuple-element.315, f32[16,512,128]{2,1,0:T(8,128)} %gather_fusion.2, pred[16]{0:T(512)(128)(4,1)S(1)} %compare_and_fusion.7, f32[512,16,512]{2,0,1:T(8,128)} %fusion.112, f32[16,512]{1,0:T(8,128)S(1)} %multiply_reduce_fusion.5, ...), kind=kOutput, calls=%fused_computation.25.clone.1 | convolution fusion | flops 6464471040 | bytes 21269008 | tf_op jit(solution)/shard_map/cond/branch_0_fun/while/body/eval_jaxpr/tjs,jsw->tw/dot_general | solution.py:19
  745.7 1.3 constant_dynamic-slice_fusion.9
  747.1 4.1 gather_fusion.3
  751.2 16.2 %fusion.112 = f32[512,16,512]{2,0,1:T(8,128)} fusion(f32[16,64,512]{2,1,0:T(8,128)S(1)} %gather_fusion.3, pred[16]{0:T(512)(128)(4,1)S(1)} %compare_and_fusion.7, f32[64,1,512]{2,1,0:T(1,128)S(1)} %constant_dynamic-slice_fusion.9, pred[]{:T(512)S(6)} %and.57), kind=kOutput, calls=%fused_computation.22.clone.1 | convolution fusion | flops 3221782528 | bytes 19005456 | tf_op jit(solution)/shard_map/cond/branch_0_fun/while/body/eval_jaxpr/dt,jds->tjs/dot_general | solution.py:14
  767.8 8.5 gather_fusion.2
  776.3 21.5 %fusion.114 = f32[4,512,128]{2,1,0:T(8,128)} fusion(f32[4,512,128]{2,1,0:T(8,128)} %get-tuple-element.316, s32[]{:T(128)} %get-tuple-element.315, f32[16,512,128]{2,1,0:T(8,128)} %gather_fusion.2, pred[16]{0:T(512)(128)(4,1)S(1)} %compare_and_fusion.7, f32[512,16,512]{2,0,1:T(8,128)} %fusion.112, f32[16,512]{1,0:T(8,128)S(1)} %multiply_reduce_fusion.5, ...), kind=kOutput, calls=%fused_computation.25.clone.1 | convolution fusion | flops 6464471040 | bytes 21269008 | tf_op jit(solution)/shard_map/cond/branch_0_fun/while/body/eval_jaxpr/tjs,jsw->tw/dot_general | solution.py:19
  797.9 2.0 broadcast.190
  799.8 2.3 constant_dynamic-update-slice_fusion
  802.1 107.5 %all-reduce.6.cloned.1.call-done = f32[6144,128]{1,0:T(8,128)} async-done(((f32[6144,128]{1,0:T(8,128)}), f32[6144,128]{1,0:T(8,128)}) %all-reduce.6.cloned.1.call-update) | async-done | bytes 3145744 | tf_op jit(solution)/shard_map/psum | solution.py:97
  909.6 3.8 copy.97
  (56 shorter events, 4.5 us)
Async XLA Ops:
  6.5 37.7 %copy-start = (f32[6144,128]{1,0:T(8,128)S(1)}, f32[6144,128]{1,0:T(8,128)}, u32[]{:S(2)}) copy-start(f32[6144,128]{1,0:T(8,128)} %param.16) | copy-start | bytes 9437188
  8.1 16.4 %all-to-all-start = ((s32[32,1,2]{2,1,0:T(1,128)}), s32[32,1,2]{2,1,0:T(1,128)S(1)}, u32[]{:S(2)}, u32[]{:S(2)}) async-start(s32[32,1,2]{2,1,0:T(1,128)} %copy.36), calls=%async_computation | async-start | bytes 32768 | tf_op jit(solution)/shard_map/all_to_all | solution.py:38
  39.1 105.0 %all-to-all-start.1 = ((f32[32,2,64,512]{3,2,1,0:T(8,128)}), f32[32,2,64,512]{3,2,1,0:T(8,128)}, u32[]{:S(2)}, u32[]{:S(2)}) async-start(f32[32,2,64,512]{3,2,1,0:T(8,128)} %broadcast_select_fusion.1), calls=%async_computation.1 | async-start | bytes 16777216 | tf_op jit(solution)/shard_map/all_to_all | solution.py:41
  144.0 434.7 %all-to-all-start.2 = ((f32[32,2,512,128]{3,2,1,0:T(8,128)}), f32[32,2,512,128]{3,2,1,0:T(8,128)}, u32[]{:S(2)}, u32[]{:S(2)}) async-start(f32[32,2,512,128]{3,2,1,0:T(8,128)} %broadcast_select_fusion), calls=%async_computation.2 | async-start | bytes 33554432 | tf_op jit(solution)/shard_map/all_to_all | solution.py:42
  155.3 3.3 copy-start.5
  155.3 294.4 %all-reduce.8.cloned.1.call-start = ((), (), s32[]{:S(2)}) async-start(), calls=%async_computation.4 | async-start | bytes 12582912 | tf_op jit(solution)/shard_map/psum | solution.py:8
  167.5 1.3 copy-start.3
  168.9 280.9 %copy-start.2 = (f32[64,6144]{1,0:T(8,128)S(1)}, f32[64,6144]{1,0:T(8,128)}, u32[]{:S(2)}) copy-start(f32[64,6144]{1,0:T(8,128)} %param.15) | copy-start | bytes 4718596
  168.9 409.9 %all-reduce.10.cloned.1.call-start = ((), (), s32[]{:S(2)}) async-start(), calls=%async_computation.5 | async-start | bytes 12582912 | tf_op jit(solution)/shard_map/psum | solution.py:9
  449.7 129.1 %copy-start.4 = (s32[12,8]{0,1:T(8,128)S(1)}, s32[12,8]{0,1:T(8,128)}, u32[]{:S(2)}) copy-start(s32[12,8]{0,1:T(8,128)} %param.20) | copy-start | bytes 1156
  449.7 459.9 %all-reduce.6.cloned.1.call-start = ((), (), s32[]{:S(2)}) async-start(), calls=%async_computation.3 | async-start | bytes 6291456 | tf_op jit(solution)/shard_map/psum | solution.py:97
  802.1 111.3 %copy-start.1 = (f32[6144,128]{1,0:T(8,128)S(1)}, f32[6144,128]{1,0:T(8,128)}, u32[]{:S(2)}) copy-start(f32[6144,128]{1,0:T(8,128)} %param.16) | copy-start | bytes 9437188
Sparse Core Ops, SparseCore 0:
  169.0 280.6 all-reduce.7
  452.1 126.6 all-reduce.9
  802.2 107.3 all-reduce.5
